TPU v7x, 32 devices: a whole 2x2x4 slice. The times are simulated.
32 devices in a mesh: grp: 2 (over core), shard: 16 (over z, y, x).
Axes of the slice: x: 2, y: 2, z: 4, core: 2. Of those that a mesh axis runs over, the one named last changes fastest.
Arguments:
- embeddings: bfloat16 [32768, 768], P(('grp', 'shard')), may hold values from -0.26 to 0.26
- centers: bfloat16 [2048, 768], P('shard'), may hold values from -0.26 to 0.26
- assignment: int32 [32768, 1], P(('grp', 'shard')), may hold values from 0 to 2047, as said below
Outputs:
- old_min: float32 [32768], P(('grp', 'shard'))
- refined_centers: float32 [2048, 768], P('shard')
- new_min: float32 [32768], P(('grp', 'shard'))
Inputs may be any that keep to these rules, and one draw needn't show every extreme that they name: `assignment`: every cluster is named by at least one row; cluster k belongs to the index of shard that holds centers[k]; the rows of one device name clusters belonging to any one index of shard at least 32 and at most 128 times, and in every group one index of shard is named 128 times by the rows of each device of that group.
All inputs are finite; a program needn't handle non-finite values.
Results may differ from a plain program's by a relative error of at most 0.0003.
Values may be sent and summed in bfloat16 or wider, within the bound.
A program may use at most 64 MiB of HBM per device.

v0:
```python
import jax
import jax.numpy as jnp
from jax import lax
from jax.sharding import PartitionSpec as P


def on_device(embeddings, centers, assignment):
    wide_rows = embeddings.astype(jnp.float32)
    row_norms = jnp.sum(jnp.square(wide_rows), 1)
    starting = jnp.full((embeddings.shape[0],), jnp.inf, jnp.float32)
    portion = lax.all_gather(centers, "shard", axis=0, tiled=True)
    portion_norms = jnp.sum(jnp.square(portion.astype(jnp.float32)), 1)
    products = lax.dot_general(
        embeddings, portion, (((1,), (1,)), ((), ())), preferred_element_type=jnp.float32
    )
    distance = row_norms[:, None] - 2.0 * products + portion_norms[None, :]
    old_min = jnp.minimum(starting, jnp.min(distance, 1))
    n_shard = lax.axis_size("shard")
    owned = centers.shape[0]
    clusters = owned * n_shard
    labels = assignment[:, 0]
    onehot = (labels[:, None] == jnp.arange(clusters, dtype=jnp.int32)[None, :]).astype(
        jnp.bfloat16
    )
    partial_totals = lax.dot_general(
        onehot, embeddings, (((0,), (0,)), ((), ())), preferred_element_type=jnp.float32
    )
    partial_counts = jnp.sum(onehot, 0, dtype=jnp.float32)
    owner_totals, owner_counts = (
        lax.psum_scatter(partial_totals, "shard", scatter_dimension=0, tiled=True),
        lax.psum_scatter(partial_counts, "shard", scatter_dimension=0, tiled=True),
    )
    totals, counts = lax.psum((owner_totals, owner_counts), "grp")
    refined_centers = totals / counts[:, None]
    portion = lax.all_gather(refined_centers, "shard", axis=0, tiled=True)
    portion_norms = jnp.sum(jnp.square(portion), 1)
    products = lax.dot_general(
        wide_rows,
        portion,
        (((1,), (1,)), ((), ())),
        precision=lax.Precision.HIGHEST,
        preferred_element_type=jnp.float32,
    )
    distance = row_norms[:, None] - 2.0 * products + portion_norms[None, :]
    new_min = jnp.minimum(starting, jnp.min(distance, 1))
    return (old_min, refined_centers, new_min)


def solution(mesh):
    placed = (P(("grp", "shard"), None), P("shard", None), P(("grp", "shard"), None))
    return jax.shard_map(
        on_device,
        mesh=mesh,
        in_specs=placed,
        out_specs=(P(("grp", "shard")), P("shard", None), P(("grp", "shard"))),
        check_vma=False,
    )
```

profile of v0, /device:TPU:0, one launch (start us, length us, event | category | flops | bytes accessed | tf_op | source)
XLA Modules:
  0.0 375.2 jit_solution(2505662859688370607)
XLA Ops:
  7.2 0.0 reduce-scatter.2.cloned.1.call-start
  7.2 7.8 %fusion.1 = f32[2048,768]{1,0:T(8,128)} fusion(bf16[1024,768]{1,0:T(8,128)(2,1)} %param.3, s32[1024]{0:T(1024)} %bitcast.7), kind=kOutput, calls=%fused_computation.4 | convolution fusion | flops 3223322624 | bytes 7868416 | tf_op jit(solution)/shard_map/dot_general | solution.py:25
  15.0 0.0 copy-start.3
  15.0 0.0 copy-start.2
  15.0 0.0 copy-start.1
  15.0 0.0 reduce-scatter.2.cloned.1.call-update
  15.1 0.0 all-reduce.3.cloned.1.call-start
  15.1 148.8 %reduce-scatter.2.cloned.1.call-done = f32[128,768]{1,0:T(8,128)} async-done(((f32[2048,768]{1,0:T(8,128)}), f32[128,768]{1,0:T(8,128)}) %reduce-scatter.2.cloned.1.call-update) | async-done | bytes 393232 | tf_op jit(solution)/shard_map/reduce_scatter | solution.py:30
  164.0 0.0 all-reduce.3.cloned.1.call-update
  164.0 0.0 all-gather.3.cloned.1.call-start
  164.0 0.7 all-gather.3.cloned.1.call-update
  164.7 0.0 all-gather.5.cloned.1.call-start
  164.8 0.0 copy-done.3
  164.8 0.6 dynamic-slice
  166.0 0.0 copy-done.2
  166.0 1.0 convert_reduce_fusion
  167.1 40.5 %all-reduce = f32[2048]{0:T(1024)S(1)} all-reduce(f32[2048]{0:T(1024)S(1)} %convert_reduce_fusion), channel_id=3, replica_groups=mesh['grp'=2,'shard'=16] {'shard'}, use_global_device_ids=true, to_apply=%region_6.0.clone | all-reduce | flops 2048 | bytes 16384
  207.6 0.1 dynamic-slice.1
  207.6 2.4 psum.15
  210.1 0.0 all-reduce.3.cloned.1.call-done
  210.1 1.8 broadcast_divide_fusion
  211.9 0.0 all-gather.5.cloned.1.call-update
  211.9 0.0 copy-done.1
  212.0 0.4 multiply_reduce_fusion.2
  212.3 44.3 %all-gather.3.cloned.1.call-done = bf16[2048,768]{1,0:T(8,128)(2,1)} async-done(((bf16[128,768]{1,0:T(8,128)(2,1)}), bf16[2048,768]{1,0:T(8,128)(2,1)}) %all-gather.3.cloned.1.call-update) | async-done | bytes 3145744 | tf_op jit(solution)/shard_map/all_gather | solution.py:11
  256.6 2.6 multiply_reduce_fusion.1
  259.2 6.4 %add_reduce_fusion.1 = f32[1024]{0:T(1024)} fusion(bf16[1024,768]{1,0:T(8,128)(2,1)S(1)} %copy-done.1, bf16[2048,768]{1,0:T(8,128)(2,1)} %all-gather.3.cloned.1.call-done, f32[2048]{0:T(1024)S(1)} %multiply_reduce_fusion.1, f32[1024]{0:T(1024)S(1)} %multiply_reduce_fusion.2), kind=kOutput, calls=%fused_computation.5 | convolution fusion | flops 3229613056 | bytes 4734976 | tf_op jit(solution)/shard_map/dot_general | solution.py:13
  265.6 87.4 %all-gather.5.cloned.1.call-done = f32[2048,768]{1,0:T(8,128)} async-done(((f32[128,768]{1,0:T(8,128)}), f32[2048,768]{1,0:T(8,128)}) %all-gather.5.cloned.1.call-update) | async-done | bytes 6291472 | tf_op jit(solution)/shard_map/all_gather | solution.py:35
  352.9 0.0 copy-start
  352.9 3.4 multiply_reduce_fusion
  356.4 1.2 copy-done
  357.5 11.1 %add_reduce_fusion = f32[1024]{0:T(1024)} fusion(f32[2048,768]{1,0:T(8,128)S(1)} %copy-done, bf16[1024,768]{1,0:T(8,128)(2,1)S(1)} %copy-done.1, f32[2048]{0:T(1024)S(1)} %multiply_reduce_fusion, f32[1024]{0:T(1024)S(1)} %multiply_reduce_fusion.2), kind=kOutput, calls=%fused_computation | convolution fusion | flops 19335741440 | bytes 7880704 | tf_op jit(solution)/shard_map/dot_general | solution.py:37
Async XLA Ops:
  7.2 156.8 %reduce-scatter.2.cloned.1.call-start = ((), (), s32[]{:S(2)}) async-start(), calls=%async_computation.2 | async-start | bytes 6684672 | tf_op jit(solution)/shard_map/reduce_scatter | solution.py:30
  15.0 149.7 %copy-start.3 = (u32[32]{0:T(128)S(1)}, u32[32]{0:T(128)}, u32[]{:S(2)}) copy-start(u32[32]{0:T(128)} %constant.9) | copy-start | bytes 388
  15.0 151.0 %copy-start.2 = (s32[1024,1]{0,1:T(1,128)S(1)}, s32[1024,1]{0,1:T(1,128)}, u32[]{:S(2)}) copy-start(s32[1024,1]{0,1:T(1,128)} %param.5) | copy-start | bytes 12292
  15.0 196.9 %copy-start.1 = (bf16[1024,768]{1,0:T(8,128)(2,1)S(1)}, bf16[1024,768]{1,0:T(8,128)(2,1)}, u32[]{:S(2)}) copy-start(bf16[1024,768]{1,0:T(8,128)(2,1)} %param.3) | copy-start | bytes 4718596
  15.1 195.0 %all-reduce.3.cloned.1.call-start = ((), (), s32[]{:S(2)}) async-start(), calls=%async_computation.3 | async-start | bytes 786432 | tf_op jit(solution)/shard_map/psum | solution.py:33
  164.0 92.7 %all-gather.3.cloned.1.call-start = ((), (), s32[]{:S(2)}) async-start(), calls=%async_computation.1 | async-start | bytes 3342336 | tf_op jit(solution)/shard_map/all_gather | solution.py:11
  164.7 188.2 %all-gather.5.cloned.1.call-start = ((), (), s32[]{:S(2)}) async-start(), calls=%async_computation.4 | async-start | bytes 6684672 | tf_op jit(solution)/shard_map/all_gather | solution.py:35
  352.9 4.6 %copy-start = (f32[2048,768]{1,0:T(8,128)S(1)}, f32[2048,768]{1,0:T(8,128)}, u32[]{:S(2)}) copy-start(f32[2048,768]{1,0:T(8,128)} %all-gather.5.cloned.1.call-done) | copy-start | bytes 18874372
Sparse Core Ops, SparseCore 0:
  15.2 148.7 reduce-scatter.1
  166.3 17.6 all-reduce.2
  187.2 69.4 all-gather.2
  260.2 92.6 all-gather.4
where the time goes:
time: 376 us; the launch traced here: 375 us
  waiting for transfers between devices  281 us (75%)
  blocking collectives  42.9 us (11%)
  matrix products  25.3 us (7%)
  between operations  14.5 us (4%)
  other arithmetic  9.24 us (2%)
    reduce_scatter x1, waiting for transfers between devices, on_device(): lax.psum_scatter(partial_totals, 'shard', scatter_dimension=0, tiled=True)  149 us
    all_gather x1, waiting for transfers between devices, on_device(): portion = lax.all_gather(refined_centers, 'shard', axis=0, tiled=True)  87.4 us
    all_gather x1, waiting for transfers between devices, on_device(): portion = lax.all_gather(centers, 'shard', axis=0, tiled=True)  44.3 us
    unnamed x1, blocking collectives  40.5 us
    dot_general x1, matrix products, on_device(): lax.dot_general(wide_rows, portion, (((1,), (1,)), ((), ())), precision=l...  11.1 us
    dot_general x1, matrix products, on_device(): lax.dot_general(onehot, embeddings, (((0,), (0,)), ((), ())), preferred_e...  7.83 us
  transfers between devices with their start and end apart: 4, of which 3 were waited for; matrix products, arithmetic and copies ran while one was open for 3% of the time, Pallas kernels for 0%

commit v1 on v0

--- a/solution.py
+++ b/solution.py
@@ -1,7 +1,286 @@
 import jax
 import jax.numpy as jnp
 from jax import lax
+from jax.experimental import pallas as pl
+from jax.experimental.pallas import tpu as pltpu
 from jax.sharding import PartitionSpec as P
+
+MESH = pl.DeviceIdType.MESH
+CHIPS = {"grp": 2, "shard": 16}
+SLICES = (2, 1, 3, 0)
+
+
+def dot_nt(left, right):
+    return lax.dot_general(
+        left, right, (((1,), (1,)), ((), ())), preferred_element_type=jnp.float32
+    )
+
+
+def square_sums(values):
+    wide = values.astype(jnp.float32)
+    square = wide * wide
+    high = square.astype(jnp.bfloat16)
+    low = (square - high.astype(jnp.float32)).astype(jnp.bfloat16)
+    ones = jnp.ones((16, values.shape[1]), jnp.bfloat16)
+    return dot_nt(ones, high) + dot_nt(ones, low)
+
+
+def kernel(
+    emb, cen, lab, old_out, refined_out, new_out,
+    tot, in1, in2, in3, rows, labels, old_all, new_all, scaled, norms,
+    halves, mine, old_acc, new_acc, local_sem, send_sem, recv_sem,
+):
+    c = lax.axis_index("grp")
+    s = lax.axis_index("shard")
+    x, y, z = s % 2, (s // 2) % 2, s // 4
+    owned, width = cen.shape
+    half = width // 2
+    n_rows = emb.shape[0]
+    x1, y1 = x + (1 - c) * (1 - 2 * x), y + c * (1 - 2 * y)
+    x2, y2 = x + c * (1 - 2 * x), y + (1 - c) * (1 - 2 * y)
+
+    def at(zz, yy, xx):
+        return zz * 4 + yy * 2 + xx
+
+    sib = (1 - c, s)
+    p1 = (c, at(z, y1, x1))
+    p2 = (c, at(z, y2, x2))
+    above = [None] + [(c, at((z + j) % 4, y, x)) for j in (1, 2, 3)]
+    cols = pl.ds(pl.multiple_of(c * half, 128), half)
+    other_cols = pl.ds(pl.multiple_of((1 - c) * half, 128), half)
+
+    sent = []
+
+    def send(src, dst, device):
+        i = len(sent)
+        copy = pltpu.make_async_remote_copy(
+            src_ref=src, dst_ref=dst, send_sem=send_sem.at[i], recv_sem=recv_sem.at[i],
+            device_id=device, device_id_type=MESH,
+        )
+        copy.start()
+        sent.append(copy)
+        return copy
+
+    barrier = pltpu.get_barrier_semaphore()
+    for peer in (sib, p1, p2, above[1], above[2], above[3]):
+        pl.semaphore_signal(barrier, inc=1, device_id=peer, device_id_type=MESH)
+    own_rows = pltpu.make_async_copy(emb.at[:, cols], rows.at[0], local_sem.at[0])
+    own_rows.start()
+    own_old = pltpu.make_async_copy(cen, old_all.at[s], local_sem.at[1])
+    own_old.start()
+    labels[0:8, :] = lab[...]
+    old_acc[...] = jnp.full(old_acc.shape, jnp.inf, jnp.float32)
+    new_acc[...] = jnp.full(new_acc.shape, jnp.inf, jnp.float32)
+    pl.semaphore_wait(barrier, 6)
+
+    rows_in = send(emb.at[:, other_cols], rows.at[1], sib)
+    labels_in = send(lab, labels.at[pl.ds(8, 8)], sib)
+
+    class Gather:
+        def __init__(self, own, buf, share_own):
+            self.buf = buf
+            spot = buf.at[s, :, cols]
+            self.z = [None] + [send(own, spot, above[j]) for j in (1, 2, 3)]
+            self.d1 = [send(own, spot, p1)]
+            self.d2 = [send(own, spot, p2)]
+            self.fz = [send(own, spot, sib) if share_own else None]
+            self.f1, self.f2, self.far, self.ffar = [], [], [], []
+
+        def spot(self, j, yy, xx):
+            return self.buf.at[at((z + 4 - j) % 4, yy, xx), :, cols]
+
+        def along_z(self):
+            for j in (1, 2, 3):
+                self.z[j].wait_recv()
+                spot = self.spot(j, y, x)
+                self.d1.append(send(spot, spot, p1))
+                self.d2.append(send(spot, spot, p2))
+                self.fz.append(send(spot, spot, sib))
+
+        def along_d1(self):
+            for j in range(4):
+                self.d1[j].wait_recv()
+                spot = self.spot(j, y1, x1)
+                self.far.append(send(spot, spot, p2))
+                self.f1.append(send(spot, spot, sib))
+
+        def along_d2(self):
+            for j in range(4):
+                self.d2[j].wait_recv()
+                spot = self.spot(j, y2, x2)
+                self.f2.append(send(spot, spot, sib))
+
+        def last(self):
+            for j in range(4):
+                self.far[j].wait_recv()
+                spot = self.spot(j, 1 - y, 1 - x)
+                self.ffar.append(send(spot, spot, sib))
+
+        def need(self, copies):
+            for copy in copies:
+                if copy is not None:
+                    copy.wait_recv()
+
+    def nearest(buf, acc, yy, xx):
+        def pair(i, carry):
+            first = at((z + 4 - 2 * i) % 4, yy, xx)
+            second = at((z + 3 - 2 * i) % 4, yy, xx)
+            block = jnp.concatenate([buf[first], buf[second]], 0)
+            distance = dot_nt(scaled[...], block) + square_sums(block)[0:1, :]
+            near = jnp.minimum(distance[:, :owned], distance[:, owned:])
+            acc[...] = jnp.minimum(acc[...], near)
+            return carry
+
+        lax.fori_loop(0, 2, pair, 0)
+
+    old = Gather(cen.at[:, cols], old_all, False)
+
+    wide = emb[...]
+    scaled[...] = wide * jnp.asarray(-2.0, jnp.bfloat16)
+    norms[...] = square_sums(wide)[0:8, :]
+
+    own_rows.wait()
+    rows_in.wait_recv()
+    labels_in.wait_recv()
+
+    def totals(j):
+        def one(f, carry):
+            fa, fb = f // 2, f % 2
+            xa = x + fa * (x1 - x) + fb * (x2 - x)
+            ya = y + fa * (y1 - y) + fb * (y2 - y)
+            base = at((z + j) % 4, ya, xa) * owned
+            ids = lax.broadcasted_iota(jnp.int32, (owned, 128), 0) + base
+            hot = [
+                (labels[r : r + 1, :] == ids).astype(jnp.float32).astype(jnp.bfloat16)
+                for r in range(16)
+            ]
+            part = jnp.zeros((owned, half), jnp.float32)
+            count = jnp.zeros((16, owned), jnp.float32)
+            ones = jnp.ones((16, n_rows), jnp.bfloat16)
+            for g in range(2):
+                block = jnp.concatenate(hot[8 * g : 8 * g + 8], 1)
+                part += jnp.dot(block, rows[g], preferred_element_type=jnp.float32)
+                count += dot_nt(ones, block)
+            tot[4 * j + f, 0:owned, :] = part
+            tot[4 * j + f, owned : owned + 8, :] = jnp.concatenate([count[0:8]] * (half // owned), 1)
+            return carry
+
+        lax.fori_loop(0, 4, one, 0)
+
+    stage1, stage2, stage3 = {}, {}, {}
+    for j in SLICES:
+        totals(j)
+        stage1[j] = send(tot.at[pl.ds(4 * j + 2, 2)], in1.at[j], p1)
+    old.along_z()
+
+    def settle(j):
+        stage2[j].wait_recv()
+        tot[4 * j] += in2[j]
+        if j > 0:
+            stage3[j] = send(tot.at[4 * j], in3.at[j - 1], above[j])
+
+    for i, j in enumerate(SLICES):
+        stage1[j].wait_recv()
+        tot[4 * j] += in1[j, 0]
+        tot[4 * j + 1] += in1[j, 1]
+        stage2[j] = send(tot.at[4 * j + 1], in2.at[j], p2)
+        if i > 0:
+            settle(SLICES[i - 1])
+    settle(SLICES[-1])
+    old.along_d1()
+
+    for j in (1, 2, 3):
+        stage3[j].wait_recv()
+    total = tot[0] + in3[0] + in3[1] + in3[2]
+    count = jnp.broadcast_to(total[owned : owned + 1, 0:owned], (owned, owned)).T
+    refined = total[0:owned, :] / jnp.concatenate([count] * (half // owned), 1)
+    halves[c] = refined
+    mine[...] = refined.astype(jnp.bfloat16)
+    own_new = pltpu.make_async_copy(mine, new_all.at[s, :, cols], local_sem.at[2])
+    own_new.start()
+    new = Gather(mine, new_all, True)
+    half_in = send(halves.at[c], halves.at[c], sib)
+
+    old.along_d2()
+    old.last()
+    own_old.wait()
+    old.need(old.fz)
+    nearest(old_all, old_acc, y, x)
+    new.along_z()
+    old.need(old.f1)
+    old.need(old.f2)
+    nearest(old_all, old_acc, y1, x1)
+    nearest(old_all, old_acc, y2, x2)
+    new.along_d1()
+    new.along_d2()
+    old.need(old.ffar)
+    nearest(old_all, old_acc, 1 - y, 1 - x)
+
+    own_new.wait()
+    new.need(new.fz)
+    nearest(new_all, new_acc, y, x)
+    new.last()
+    new.need(new.f1)
+    new.need(new.f2)
+    nearest(new_all, new_acc, y1, x1)
+    nearest(new_all, new_acc, y2, x2)
+    half_in.wait_recv()
+    refined_out[:, 0:half] = halves[0]
+    refined_out[:, half:width] = halves[1]
+    old_out[...] = jnp.min(old_acc[...].T, 0, keepdims=True) + norms[0:1, :]
+    new.need(new.ffar)
+    nearest(new_all, new_acc, 1 - y, 1 - x)
+    new_out[...] = jnp.min(new_acc[...].T, 0, keepdims=True) + norms[0:1, :]
+    for copy in sent:
+        copy.wait_send()
+
+
+COPIES = 80
+
+
+def in_one_kernel(embeddings, centers, assignment):
+    n_rows, width = embeddings.shape
+    owned = centers.shape[0]
+    half = width // 2
+    f32, bf16 = jnp.float32, jnp.bfloat16
+    vmem = pl.BlockSpec(memory_space=pltpu.VMEM)
+    old_min, refined, new_min = pl.pallas_call(
+        kernel,
+        out_shape=(
+            jax.ShapeDtypeStruct((1, n_rows), f32),
+            jax.ShapeDtypeStruct((owned, width), f32),
+            jax.ShapeDtypeStruct((1, n_rows), f32),
+        ),
+        in_specs=[vmem] * 3,
+        out_specs=(vmem,) * 3,
+        scratch_shapes=[
+            pltpu.VMEM((16, owned + 8, half), f32),
+            pltpu.VMEM((4, 2, owned + 8, half), f32),
+            pltpu.VMEM((4, owned + 8, half), f32),
+            pltpu.VMEM((3, owned + 8, half), f32),
+            pltpu.VMEM((2, n_rows, half), bf16),
+            pltpu.VMEM((16, 128), jnp.int32),
+            pltpu.VMEM((16, owned, width), bf16),
+            pltpu.VMEM((16, owned, width), bf16),
+            pltpu.VMEM((n_rows, width), bf16),
+            pltpu.VMEM((8, n_rows), f32),
+            pltpu.VMEM((2, owned, half), f32),
+            pltpu.VMEM((owned, half), bf16),
+            pltpu.VMEM((n_rows, owned), f32),
+            pltpu.VMEM((n_rows, owned), f32),
+            pltpu.SemaphoreType.DMA((3,)),
+            pltpu.SemaphoreType.DMA((COPIES,)),
+            pltpu.SemaphoreType.DMA((COPIES,)),
+        ],
+        compiler_params=pltpu.CompilerParams(
+            collective_id=0, has_side_effects=True, vmem_limit_bytes=48 * 1024 * 1024
+        ),
+        cost_estimate=pl.CostEstimate(
+            flops=6 * n_rows * 16 * owned * width, bytes_accessed=8 * n_rows * width, transcendentals=0
+        ),
+        name="lloyd_step",
+    )(embeddings, centers, assignment.reshape(n_rows // 128, 128))
+    return old_min.reshape(n_rows), refined, new_min.reshape(n_rows)
 
 
 def on_device(embeddings, centers, assignment):
@@ -48,8 +327,9 @@
 
 def solution(mesh):
     placed = (P(("grp", "shard"), None), P("shard", None), P(("grp", "shard"), None))
+    here = dict(mesh.shape) == CHIPS
     return jax.shard_map(
-        on_device,
+        in_one_kernel if here else on_device,
         mesh=mesh,
         in_specs=placed,
         out_specs=(P(("grp", "shard")), P("shard", None), P(("grp", "shard"))),

time: 376 us -> 79.9 us (0.21)
  waiting for transfers between devices: 281 us -> 0 us
  Pallas kernels: 0 us -> 74.1 us
  blocking collectives: 42.9 us -> 0 us
  matrix products: 25.3 us -> 0 us
  between operations: 14.5 us -> 0.65 us
  other arithmetic: 9.24 us -> 0 us
    reduce_scatter x1 -> x0, waiting for transfers between devices: 149 us -> none  [on_device(): lax.psum_scatter(partial_totals, 'shard', scatter_dimension=0, tiled=True)]
    all_gather x2 -> x0, waiting for transfers between devices: 132 us -> none  [the longest x1 87.4 us: on_device(): portion = lax.all_gather(refined_centers, 'shard', axis=0, tiled=True)]
    pallas_call x0 -> x1, Pallas kernels: none -> 74.1 us  [in_one_kernel(): pl.pallas_call(kernel, out_shape=(jax.ShapeDtypeStruct((1, n_rows), f32),...]
    unnamed x1 -> x0, blocking collectives: 40.5 us -> none
    dot_general x3 -> x0, matrix products: 25.3 us -> none  [the longest x1 11.1 us: on_device(): lax.dot_general(wide_rows, portion, (((1,), (1,)), ((), ())), precision=l...]
    reduce_sum x4 -> x0, other arithmetic: 7.4 us -> none  [the longest x1 3.42 us: on_device(): portion_norms = jnp.sum(jnp.square(portion), 1)]
  transfers between devices with their start and end apart: 4 -> 0, of which waited for: 3 -> 0; matrix products, arithmetic and copies ran while one was open for 3% -> 0% of each run, Pallas kernels for 0% -> 0%
where the time goes in v1:
time: 79.9 us; the launch traced here: 79.7 us
  Pallas kernels  74.1 us (93%)
  local copies, waits for them, and re-layouts  4.95 us (6%)
    pallas_call x1, Pallas kernels, in_one_kernel(): pl.pallas_call(kernel, out_shape=(jax.ShapeDtypeStruct((1, n_rows), f32),...  74.1 us
    unnamed x9, local copies, waits for them, and re-layouts  4.95 us

profile of v1, /device:TPU:0, one launch (start us, length us, event | category | flops | bytes accessed | tf_op | source)
XLA Modules:
  0.0 79.7 jit_solution(3813096000046785659)
XLA Ops:
  0.6 0.0 copy-start
  0.6 1.4 %copy-done = bf16[1024,768]{1,0:T(8,128)(2,1)S(1)} copy-done((bf16[1024,768]{1,0:T(8,128)(2,1)S(1)}, bf16[1024,768]{1,0:T(8,128)(2,1)}, u32[]{:S(2)}) %copy-start) | copy-done | bytes 1572888
  2.0 0.0 copy-start.1
  2.0 0.9 %copy-done.1 = bf16[128,768]{1,0:T(8,128)(2,1)S(1)} copy-done((bf16[128,768]{1,0:T(8,128)(2,1)S(1)}, bf16[128,768]{1,0:T(8,128)(2,1)}, u32[]{:S(2)}) %copy-start.1) | copy-done | bytes 196632
  3.0 0.0 copy-start.2
  3.0 0.7 copy-done.2
  3.7 74.1 %lloyd_step.1 = (f32[1,1024]{1,0:T(1,128)S(1)}, f32[128,768]{1,0:T(8,128)S(1)}, f32[1,1024]{1,0:T(1,128)S(1)}) custom-call(bf16[1024,768]{1,0:T(8,128)(2,1)S(1)} %copy-done, bf16[128,768]{1,0:T(8,128)(2,1)S(1)} %copy-done.1, s32[8,128]{1,0:T(8,128)S(1)} %bitcast.5), custom_call_target="tpu_custom_call" | custom-call | flops 9663676416 | bytes 6291456 | tf_op jit(solution)/shard_map/lloyd_step/pallas_call | solution.py:247
  77.8 0.6 copy.9
  78.4 0.7 copy.10
  79.1 0.6 copy.11
Async XLA Ops:
  0.6 1.4 %copy-start = (bf16[1024,768]{1,0:T(8,128)(2,1)S(1)}, bf16[1024,768]{1,0:T(8,128)(2,1)}, u32[]{:S(2)}) copy-start(bf16[1024,768]{1,0:T(8,128)(2,1)} %emb.1) | copy-start | bytes 4718596
  2.0 0.9 %copy-start.1 = (bf16[128,768]{1,0:T(8,128)(2,1)S(1)}, bf16[128,768]{1,0:T(8,128)(2,1)}, u32[]{:S(2)}) copy-start(bf16[128,768]{1,0:T(8,128)(2,1)} %cen.1) | copy-start | bytes 589828
  3.0 0.7 copy-start.2

commit v2 on v1

--- a/solution.py
+++ b/solution.py
@@ -25,9 +25,31 @@
     return dot_nt(ones, high) + dot_nt(ones, low)
 
 
+def column(row):
+    return jnp.broadcast_to(row, (128, 128)).T
+
+
+def pack(block, whole, meta):
+    half = whole.shape[1]
+    values, count = block[:, 0:half], block[:, half:]
+    most = jnp.maximum(jnp.max(jnp.abs(values), 1, keepdims=True), 1e-30)
+    whole[...] = jnp.round(values * (32767.0 / most)).astype(jnp.int32).astype(jnp.int16)
+    scale = jnp.broadcast_to(most * (1.0 / 32767.0), count.shape)
+    lane = lax.broadcasted_iota(jnp.int32, count.shape, 1)
+    meta[...] = jnp.where(lane < 4, count, scale).T[0:8]
+
+
+def unpack(whole, meta):
+    half = whole.shape[1]
+    count, scale = column(meta[0:1, :]), column(meta[4:5, :])
+    values = whole[...].astype(jnp.int32).astype(jnp.float32)
+    return jnp.concatenate([values * jnp.concatenate([scale] * (half // 128), 1), count], 1)
+
+
 def kernel(
     emb, cen, lab, old_out, refined_out, new_out,
-    tot, in1, in2, in3, rows, labels, old_all, new_all, scaled, norms,
+    tot, out1, meta1, in1, min1, out2, meta2, in2, min2, out3, meta3, in3, min3,
+    rows, labels, old_all, new_all, here, scaled, norms,
     halves, mine, old_acc, new_acc, local_sem, send_sem, recv_sem,
 ):
     c = lax.axis_index("grp")
@@ -64,16 +86,20 @@
     barrier = pltpu.get_barrier_semaphore()
     for peer in (sib, p1, p2, above[1], above[2], above[3]):
         pl.semaphore_signal(barrier, inc=1, device_id=peer, device_id_type=MESH)
-    own_rows = pltpu.make_async_copy(emb.at[:, cols], rows.at[0], local_sem.at[0])
+    own_lab = pltpu.make_async_copy(lab, labels.at[pl.ds(0, 8)], local_sem.at[3])
+    own_lab.start()
+    own_emb = pltpu.make_async_copy(emb, here, local_sem.at[4])
+    own_emb.start()
+    own_rows = pltpu.make_async_copy(emb.at[:, cols], rows.at[0, :, pl.ds(0, half)], local_sem.at[0])
     own_rows.start()
     own_old = pltpu.make_async_copy(cen, old_all.at[s], local_sem.at[1])
     own_old.start()
-    labels[0:8, :] = lab[...]
+    rows[:, :, half:] = jnp.ones((2, n_rows, 128), jnp.bfloat16)
     old_acc[...] = jnp.full(old_acc.shape, jnp.inf, jnp.float32)
     new_acc[...] = jnp.full(new_acc.shape, jnp.inf, jnp.float32)
     pl.semaphore_wait(barrier, 6)
 
-    rows_in = send(emb.at[:, other_cols], rows.at[1], sib)
+    rows_in = send(emb.at[:, other_cols], rows.at[1, :, pl.ds(0, half)], sib)
     labels_in = send(lab, labels.at[pl.ds(8, 8)], sib)
 
     class Gather:
@@ -135,65 +161,84 @@
 
     old = Gather(cen.at[:, cols], old_all, False)
 
-    wide = emb[...]
+    own_emb.wait()
+    wide = here[...]
     scaled[...] = wide * jnp.asarray(-2.0, jnp.bfloat16)
     norms[...] = square_sums(wide)[0:8, :]
 
+    own_lab.wait()
     own_rows.wait()
     rows_in.wait_recv()
     labels_in.wait_recv()
 
-    def totals(j):
-        def one(f, carry):
-            fa, fb = f // 2, f % 2
-            xa = x + fa * (x1 - x) + fb * (x2 - x)
-            ya = y + fa * (y1 - y) + fb * (y2 - y)
-            base = at((z + j) % 4, ya, xa) * owned
-            ids = lax.broadcasted_iota(jnp.int32, (owned, 128), 0) + base
-            hot = [
-                (labels[r : r + 1, :] == ids).astype(jnp.float32).astype(jnp.bfloat16)
-                for r in range(16)
-            ]
-            part = jnp.zeros((owned, half), jnp.float32)
-            count = jnp.zeros((16, owned), jnp.float32)
-            ones = jnp.ones((16, n_rows), jnp.bfloat16)
-            for g in range(2):
-                block = jnp.concatenate(hot[8 * g : 8 * g + 8], 1)
-                part += jnp.dot(block, rows[g], preferred_element_type=jnp.float32)
-                count += dot_nt(ones, block)
-            tot[4 * j + f, 0:owned, :] = part
-            tot[4 * j + f, owned : owned + 8, :] = jnp.concatenate([count[0:8]] * (half // owned), 1)
+    def partial(j, fa, fb):
+        xa = x + fa * (x1 - x) + fb * (x2 - x)
+        ya = y + fa * (y1 - y) + fb * (y2 - y)
+        base = at((z + j) % 4, ya, xa) * owned
+        ids = lax.broadcasted_iota(jnp.int32, (owned, 128), 0) + base
+        hot = [
+            (labels[r : r + 1, :] == ids).astype(jnp.float32).astype(jnp.bfloat16)
+            for r in range(16)
+        ]
+        part = jnp.zeros((owned, half + 128), jnp.float32)
+        for g in range(2):
+            block = jnp.concatenate(hot[8 * g : 8 * g + 8], 1)
+            part += jnp.dot(block, rows[g], preferred_element_type=jnp.float32)
+        return part
+
+    stage1, stage2, stage3 = {}, {}, {}
+
+    def begin(j):
+        def away(fb, carry):
+            pack(partial(j, 1, fb), out1.at[j, fb], meta1.at[j, fb])
             return carry
 
-        lax.fori_loop(0, 4, one, 0)
-
-    stage1, stage2, stage3 = {}, {}, {}
-    for j in SLICES:
-        totals(j)
-        stage1[j] = send(tot.at[pl.ds(4 * j + 2, 2)], in1.at[j], p1)
+        def kept(fb, carry):
+            tot[2 * j + fb] = partial(j, 0, fb)
+            return carry
+
+        lax.fori_loop(0, 2, away, 0)
+        stage1[j] = (send(out1.at[j], in1.at[j], p1), send(meta1.at[j], min1.at[j], p1))
+        lax.fori_loop(0, 2, kept, 0)
+
+    def middle(j):
+        for copy in stage1[j]:
+            copy.wait_recv()
+        pack(tot[2 * j + 1] + unpack(in1.at[j, 1], min1.at[j, 1]), out2.at[j], meta2.at[j])
+        stage2[j] = (send(out2.at[j], in2.at[j], p2), send(meta2.at[j], min2.at[j], p2))
+        tot[2 * j] += unpack(in1.at[j, 0], min1.at[j, 0])
+
+    def settle(j):
+        for copy in stage2[j]:
+            copy.wait_recv()
+        tot[2 * j] += unpack(in2.at[j], min2.at[j])
+        if j > 0:
+            i = j - 1
+            pack(tot[2 * j], out3.at[i], meta3.at[i])
+            stage3[j] = (send(out3.at[i], in3.at[i], above[j]), send(meta3.at[i], min3.at[i], above[j]))
+
+    begin(SLICES[0])
+    begin(SLICES[1])
     old.along_z()
-
-    def settle(j):
-        stage2[j].wait_recv()
-        tot[4 * j] += in2[j]
-        if j > 0:
-            stage3[j] = send(tot.at[4 * j], in3.at[j - 1], above[j])
-
-    for i, j in enumerate(SLICES):
-        stage1[j].wait_recv()
-        tot[4 * j] += in1[j, 0]
-        tot[4 * j + 1] += in1[j, 1]
-        stage2[j] = send(tot.at[4 * j + 1], in2.at[j], p2)
-        if i > 0:
-            settle(SLICES[i - 1])
-    settle(SLICES[-1])
+    middle(SLICES[0])
+    begin(SLICES[2])
+    middle(SLICES[1])
+    settle(SLICES[0])
+    begin(SLICES[3])
+    middle(SLICES[2])
+    settle(SLICES[1])
     old.along_d1()
-
-    for j in (1, 2, 3):
-        stage3[j].wait_recv()
-    total = tot[0] + in3[0] + in3[1] + in3[2]
-    count = jnp.broadcast_to(total[owned : owned + 1, 0:owned], (owned, owned)).T
-    refined = total[0:owned, :] / jnp.concatenate([count] * (half // owned), 1)
+    middle(SLICES[3])
+    settle(SLICES[2])
+    settle(SLICES[3])
+    old.along_d2()
+
+    total = tot[0]
+    for j in SLICES[:3]:
+        for copy in stage3[j]:
+            copy.wait_recv()
+        total += unpack(in3.at[j - 1], min3.at[j - 1])
+    refined = total[:, 0:half] / jnp.concatenate([total[:, half:]] * (half // 128), 1)
     halves[c] = refined
     mine[...] = refined.astype(jnp.bfloat16)
     own_new = pltpu.make_async_copy(mine, new_all.at[s, :, cols], local_sem.at[2])
@@ -201,7 +246,6 @@
     new = Gather(mine, new_all, True)
     half_in = send(halves.at[c], halves.at[c], sib)
 
-    old.along_d2()
     old.last()
     own_old.wait()
     old.need(old.fz)
@@ -235,14 +279,14 @@
         copy.wait_send()
 
 
-COPIES = 80
+COPIES = 96
 
 
 def in_one_kernel(embeddings, centers, assignment):
     n_rows, width = embeddings.shape
     owned = centers.shape[0]
     half = width // 2
-    f32, bf16 = jnp.float32, jnp.bfloat16
+    f32, bf16, i16 = jnp.float32, jnp.bfloat16, jnp.int16
     vmem = pl.BlockSpec(memory_space=pltpu.VMEM)
     old_min, refined, new_min = pl.pallas_call(
         kernel,
@@ -251,24 +295,34 @@
             jax.ShapeDtypeStruct((owned, width), f32),
             jax.ShapeDtypeStruct((1, n_rows), f32),
         ),
-        in_specs=[vmem] * 3,
+        in_specs=[pl.BlockSpec(memory_space=pl.ANY)] * 3,
         out_specs=(vmem,) * 3,
         scratch_shapes=[
-            pltpu.VMEM((16, owned + 8, half), f32),
-            pltpu.VMEM((4, 2, owned + 8, half), f32),
-            pltpu.VMEM((4, owned + 8, half), f32),
-            pltpu.VMEM((3, owned + 8, half), f32),
-            pltpu.VMEM((2, n_rows, half), bf16),
+            pltpu.VMEM((8, owned, half + 128), f32),
+            pltpu.VMEM((4, 2, owned, half), i16),
+            pltpu.VMEM((4, 2, 8, 128), f32),
+            pltpu.VMEM((4, 2, owned, half), i16),
+            pltpu.VMEM((4, 2, 8, 128), f32),
+            pltpu.VMEM((4, owned, half), i16),
+            pltpu.VMEM((4, 8, 128), f32),
+            pltpu.VMEM((4, owned, half), i16),
+            pltpu.VMEM((4, 8, 128), f32),
+            pltpu.VMEM((3, owned, half), i16),
+            pltpu.VMEM((3, 8, 128), f32),
+            pltpu.VMEM((3, owned, half), i16),
+            pltpu.VMEM((3, 8, 128), f32),
+            pltpu.VMEM((2, n_rows, half + 128), bf16),
             pltpu.VMEM((16, 128), jnp.int32),
             pltpu.VMEM((16, owned, width), bf16),
             pltpu.VMEM((16, owned, width), bf16),
+            pltpu.VMEM((n_rows, width), bf16),
             pltpu.VMEM((n_rows, width), bf16),
             pltpu.VMEM((8, n_rows), f32),
             pltpu.VMEM((2, owned, half), f32),
             pltpu.VMEM((owned, half), bf16),
             pltpu.VMEM((n_rows, owned), f32),
             pltpu.VMEM((n_rows, owned), f32),
-            pltpu.SemaphoreType.DMA((3,)),
+            pltpu.SemaphoreType.DMA((5,)),
             pltpu.SemaphoreType.DMA((COPIES,)),
             pltpu.SemaphoreType.DMA((COPIES,)),
         ],

time: 79.9 us -> 68.5 us (0.86)
  Pallas kernels: 74.1 us -> 62.8 us
    pallas_call x1, Pallas kernels: 74.1 us -> 62.8 us  [in_one_kernel(): pl.pallas_call(kernel, out_shape=(jax.ShapeDtypeStruct((1, n_rows), f32),...]
where the time goes in v2:
time: 68.5 us; the launch traced here: 68.3 us
  Pallas kernels  62.8 us (92%)
  local copies, waits for them, and re-layouts  4.95 us (7%)
    pallas_call x1, Pallas kernels, in_one_kernel(): pl.pallas_call(kernel, out_shape=(jax.ShapeDtypeStruct((1, n_rows), f32),...  62.8 us
    unnamed x9, local copies, waits for them, and re-layouts  4.95 us

profile of v2, /device:TPU:0, one launch (start us, length us, event | category | flops | bytes accessed | tf_op | source)
XLA Modules:
  0.0 68.3 jit_solution(10916462712761240662)
XLA Ops:
  0.6 0.0 copy-start
  0.6 1.4 %copy-done = bf16[1024,768]{1,0:T(8,128)(2,1)S(1)} copy-done((bf16[1024,768]{1,0:T(8,128)(2,1)S(1)}, bf16[1024,768]{1,0:T(8,128)(2,1)}, u32[]{:S(2)}) %copy-start) | copy-done | bytes 1572888
  2.0 0.0 copy-start.1
  2.0 0.9 %copy-done.1 = bf16[128,768]{1,0:T(8,128)(2,1)S(1)} copy-done((bf16[128,768]{1,0:T(8,128)(2,1)S(1)}, bf16[128,768]{1,0:T(8,128)(2,1)}, u32[]{:S(2)}) %copy-start.1) | copy-done | bytes 196632
  3.0 0.0 copy-start.2
  3.0 0.7 %copy-done.2 = s32[1024,1]{0,1:T(1,128)S(1)} copy-done((s32[1024,1]{0,1:T(1,128)S(1)}, s32[1024,1]{0,1:T(1,128)}, u32[]{:S(2)}) %copy-start.2) | copy-done | bytes 4120
  3.7 62.8 %lloyd_step.1 = (f32[1,1024]{1,0:T(1,128)S(1)}, f32[128,768]{1,0:T(8,128)S(1)}, f32[1,1024]{1,0:T(1,128)S(1)}) custom-call(bf16[1024,768]{1,0:T(8,128)(2,1)S(1)} %copy-done, bf16[128,768]{1,0:T(8,128)(2,1)S(1)} %copy-done.1, s32[8,128]{1,0:T(8,128)S(1)} %bitcast.5), custom_call_target="tpu_custom_call" | custom-call | flops 9663676416 | bytes 6291456 | tf_op jit(solution)/shard_map/lloyd_step/pallas_call | solution.py:291
  66.4 0.6 copy.9
  67.0 0.7 %copy.10 = f32[128,768]{1,0:T(8,128)} copy(f32[128,768]{1,0:T(8,128)S(1)} %get-tuple-element.13) | data formatting | bytes 786432
  67.8 0.6 copy.11
Async XLA Ops:
  0.6 1.4 %copy-start = (bf16[1024,768]{1,0:T(8,128)(2,1)S(1)}, bf16[1024,768]{1,0:T(8,128)(2,1)}, u32[]{:S(2)}) copy-start(bf16[1024,768]{1,0:T(8,128)(2,1)} %emb.1) | copy-start | bytes 4718596
  2.0 0.9 %copy-start.1 = (bf16[128,768]{1,0:T(8,128)(2,1)S(1)}, bf16[128,768]{1,0:T(8,128)(2,1)}, u32[]{:S(2)}) copy-start(bf16[128,768]{1,0:T(8,128)(2,1)} %cen.1) | copy-start | bytes 589828
  3.0 0.7 %copy-start.2 = (s32[1024,1]{0,1:T(1,128)S(1)}, s32[1024,1]{0,1:T(1,128)}, u32[]{:S(2)}) copy-start(s32[1024,1]{0,1:T(1,128)} %param.5) | copy-start | bytes 12292

commit v3 on v2

--- a/solution.py
+++ b/solution.py
@@ -7,7 +7,7 @@
 
 MESH = pl.DeviceIdType.MESH
 CHIPS = {"grp": 2, "shard": 16}
-SLICES = (2, 1, 3, 0)
+SLICES = (3, 2, 1, 0)
 
 
 def dot_nt(left, right):
@@ -64,10 +64,14 @@
     def at(zz, yy, xx):
         return zz * 4 + yy * 2 + xx
 
+    def level(j):
+        far = (z + 2 * (j // 2)) % 4
+        return far + (j % 2) * (1 - 2 * (far % 2))
+
     sib = (1 - c, s)
     p1 = (c, at(z, y1, x1))
     p2 = (c, at(z, y2, x2))
-    above = [None] + [(c, at((z + j) % 4, y, x)) for j in (1, 2, 3)]
+    above = [None] + [(c, at(level(j), y, x)) for j in (1, 2, 3)]
     cols = pl.ds(pl.multiple_of(c * half, 128), half)
     other_cols = pl.ds(pl.multiple_of((1 - c) * half, 128), half)
 
@@ -113,31 +117,31 @@
             self.f1, self.f2, self.far, self.ffar = [], [], [], []
 
         def spot(self, j, yy, xx):
-            return self.buf.at[at((z + 4 - j) % 4, yy, xx), :, cols]
-
-        def along_z(self):
-            for j in (1, 2, 3):
+            return self.buf.at[at(level(j), yy, xx), :, cols]
+
+        def along_z(self, *which):
+            for j in which:
                 self.z[j].wait_recv()
                 spot = self.spot(j, y, x)
                 self.d1.append(send(spot, spot, p1))
                 self.d2.append(send(spot, spot, p2))
                 self.fz.append(send(spot, spot, sib))
 
-        def along_d1(self):
-            for j in range(4):
+        def along_d1(self, *which):
+            for j in which:
                 self.d1[j].wait_recv()
                 spot = self.spot(j, y1, x1)
                 self.far.append(send(spot, spot, p2))
                 self.f1.append(send(spot, spot, sib))
 
-        def along_d2(self):
-            for j in range(4):
+        def along_d2(self, *which):
+            for j in which:
                 self.d2[j].wait_recv()
                 spot = self.spot(j, y2, x2)
                 self.f2.append(send(spot, spot, sib))
 
-        def last(self):
-            for j in range(4):
+        def last(self, *which):
+            for j in which:
                 self.far[j].wait_recv()
                 spot = self.spot(j, 1 - y, 1 - x)
                 self.ffar.append(send(spot, spot, sib))
@@ -147,59 +151,55 @@
                 if copy is not None:
                     copy.wait_recv()
 
-    def nearest(buf, acc, yy, xx):
+    def nearest(buf, acc, yy, xx, start=0, stop=2):
         def pair(i, carry):
-            first = at((z + 4 - 2 * i) % 4, yy, xx)
-            second = at((z + 3 - 2 * i) % 4, yy, xx)
+            far = (z + 2 * i) % 4
+            first = at(far, yy, xx)
+            second = at(far + 1 - 2 * (far % 2), yy, xx)
             block = jnp.concatenate([buf[first], buf[second]], 0)
             distance = dot_nt(scaled[...], block) + square_sums(block)[0:1, :]
             near = jnp.minimum(distance[:, :owned], distance[:, owned:])
             acc[...] = jnp.minimum(acc[...], near)
             return carry
 
-        lax.fori_loop(0, 2, pair, 0)
+        lax.fori_loop(start, stop, pair, 0)
 
     old = Gather(cen.at[:, cols], old_all, False)
-
-    own_emb.wait()
-    wide = here[...]
-    scaled[...] = wide * jnp.asarray(-2.0, jnp.bfloat16)
-    norms[...] = square_sums(wide)[0:8, :]
 
     own_lab.wait()
     own_rows.wait()
     rows_in.wait_recv()
     labels_in.wait_recv()
 
-    def partial(j, fa, fb):
-        xa = x + fa * (x1 - x) + fb * (x2 - x)
-        ya = y + fa * (y1 - y) + fb * (y2 - y)
-        base = at((z + j) % 4, ya, xa) * owned
-        ids = lax.broadcasted_iota(jnp.int32, (owned, 128), 0) + base
-        hot = [
-            (labels[r : r + 1, :] == ids).astype(jnp.float32).astype(jnp.bfloat16)
-            for r in range(16)
-        ]
-        part = jnp.zeros((owned, half + 128), jnp.float32)
-        for g in range(2):
-            block = jnp.concatenate(hot[8 * g : 8 * g + 8], 1)
-            part += jnp.dot(block, rows[g], preferred_element_type=jnp.float32)
-        return part
+    def partial(j, fa):
+        hot = []
+        for fb in range(2):
+            xa = x + fa * (x1 - x) + fb * (x2 - x)
+            ya = y + fa * (y1 - y) + fb * (y2 - y)
+            hot.append(lax.broadcasted_iota(jnp.int32, (owned, 128), 0) + at(level(j), ya, xa) * owned)
+        ids = jnp.concatenate(hot, 0)
+
+        def one(g, part):
+            hot = [
+                (labels[pl.ds(8 * g + r, 1), :] == ids).astype(jnp.float32).astype(jnp.bfloat16)
+                for r in range(8)
+            ]
+            block = jnp.concatenate(hot, 1)
+            return part + jnp.dot(block, rows[g], preferred_element_type=jnp.float32)
+
+        part = one(0, jnp.zeros((2 * owned, half + 128), jnp.float32))
+        return one(1, part)
 
     stage1, stage2, stage3 = {}, {}, {}
 
     def begin(j):
-        def away(fb, carry):
-            pack(partial(j, 1, fb), out1.at[j, fb], meta1.at[j, fb])
-            return carry
-
-        def kept(fb, carry):
-            tot[2 * j + fb] = partial(j, 0, fb)
-            return carry
-
-        lax.fori_loop(0, 2, away, 0)
+        part = partial(j, 1)
+        for fb in range(2):
+            pack(part[fb * owned : (fb + 1) * owned], out1.at[j, fb], meta1.at[j, fb])
         stage1[j] = (send(out1.at[j], in1.at[j], p1), send(meta1.at[j], min1.at[j], p1))
-        lax.fori_loop(0, 2, kept, 0)
+        part = partial(j, 0)
+        for fb in range(2):
+            tot[2 * j + fb] = part[fb * owned : (fb + 1) * owned]
 
     def middle(j):
         for copy in stage1[j]:
@@ -219,7 +219,12 @@
 
     begin(SLICES[0])
     begin(SLICES[1])
-    old.along_z()
+    old.along_z(1, 2, 3)
+    own_emb.wait()
+    wide = here[...]
+    scaled[...] = wide * jnp.asarray(-2.0, jnp.bfloat16)
+    norms[...] = square_sums(wide)[0:8, :]
+
     middle(SLICES[0])
     begin(SLICES[2])
     middle(SLICES[1])
@@ -227,11 +232,11 @@
     begin(SLICES[3])
     middle(SLICES[2])
     settle(SLICES[1])
-    old.along_d1()
+    old.along_d1(0, 1, 2, 3)
     middle(SLICES[3])
     settle(SLICES[2])
     settle(SLICES[3])
-    old.along_d2()
+    old.along_d2(0, 1, 2, 3)
 
     total = tot[0]
     for j in SLICES[:3]:
@@ -246,40 +251,52 @@
     new = Gather(mine, new_all, True)
     half_in = send(halves.at[c], halves.at[c], sib)
 
-    old.last()
     own_old.wait()
     old.need(old.fz)
     nearest(old_all, old_acc, y, x)
-    new.along_z()
-    old.need(old.f1)
-    old.need(old.f2)
+    new.along_z(1)
+    old.last(0, 1, 2, 3)
+    new.along_z(2)
+    old.need(old.f1 + old.f2)
     nearest(old_all, old_acc, y1, x1)
+    new.along_z(3)
+    new.along_d1(0, 1)
     nearest(old_all, old_acc, y2, x2)
-    new.along_d1()
-    new.along_d2()
+    new.along_d1(2, 3)
+    new.along_d2(0, 1, 2, 3)
     old.need(old.ffar)
     nearest(old_all, old_acc, 1 - y, 1 - x)
-
+    new.last(0, 1)
+    old_out[...] = jnp.min(old_acc[...].T, 0, keepdims=True) + norms[0:1, :]
+    half_in.wait_recv()
+    refined_out[:, 0:half] = halves[0]
+    refined_out[:, half:width] = halves[1]
     own_new.wait()
     new.need(new.fz)
     nearest(new_all, new_acc, y, x)
-    new.last()
-    new.need(new.f1)
-    new.need(new.f2)
+    new.last(2, 3)
+    new.need(new.f1 + new.f2)
     nearest(new_all, new_acc, y1, x1)
     nearest(new_all, new_acc, y2, x2)
-    half_in.wait_recv()
-    refined_out[:, 0:half] = halves[0]
-    refined_out[:, half:width] = halves[1]
-    old_out[...] = jnp.min(old_acc[...].T, 0, keepdims=True) + norms[0:1, :]
-    new.need(new.ffar)
-    nearest(new_all, new_acc, 1 - y, 1 - x)
+    new.need(new.ffar[:2])
+    nearest(new_all, new_acc, 1 - y, 1 - x, 0, 1)
+    new.need(new.ffar[2:])
+    nearest(new_all, new_acc, 1 - y, 1 - x, 1, 2)
     new_out[...] = jnp.min(new_acc[...].T, 0, keepdims=True) + norms[0:1, :]
     for copy in sent:
         copy.wait_send()
 
 
 COPIES = 96
+
+
+def write_out(old_min, refined, new_min, old_out, refined_out, new_out, sems):
+    pairs = ((old_min, old_out), (refined, refined_out), (new_min, new_out))
+    copies = [pltpu.make_async_copy(src, dst, sems.at[i]) for i, (src, dst) in enumerate(pairs)]
+    for copy in copies:
+        copy.start()
+    for copy in copies:
+        copy.wait()
 
 
 def in_one_kernel(embeddings, centers, assignment):
@@ -327,13 +344,24 @@
             pltpu.SemaphoreType.DMA((COPIES,)),
         ],
         compiler_params=pltpu.CompilerParams(
-            collective_id=0, has_side_effects=True, vmem_limit_bytes=48 * 1024 * 1024
+            collective_id=0, has_side_effects=True, vmem_limit_bytes=60 * 1024 * 1024
         ),
         cost_estimate=pl.CostEstimate(
             flops=6 * n_rows * 16 * owned * width, bytes_accessed=8 * n_rows * width, transcendentals=0
         ),
         name="lloyd_step",
     )(embeddings, centers, assignment.reshape(n_rows // 128, 128))
+    outs = (old_min, refined, new_min)
+    anywhere = pl.BlockSpec(memory_space=pl.ANY)
+    old_min, refined, new_min = pl.pallas_call(
+        write_out,
+        out_shape=tuple(jax.ShapeDtypeStruct(out.shape, f32) for out in outs),
+        in_specs=[anywhere] * 3,
+        out_specs=(anywhere,) * 3,
+        scratch_shapes=[pltpu.SemaphoreType.DMA((3,))],
+        compiler_params=pltpu.CompilerParams(vmem_limit_bytes=60 * 1024 * 1024),
+        name="write_out",
+    )(*outs)
     return old_min.reshape(n_rows), refined, new_min.reshape(n_rows)
 
 

time: 68.5 us -> 75.9 us (1.11)
  Pallas kernels: 62.8 us -> 74.9 us
  local copies, waits for them, and re-layouts: 4.95 us -> 0 us
    pallas_call x0 -> x1, Pallas kernels: none -> 13.3 us  [in_one_kernel(): pl.pallas_call(write_out, out_shape=tuple((jax.ShapeDtypeStruct(out.shape...]
    unnamed x9 -> x0, local copies, waits for them, and re-layouts: 4.95 us -> none
    pallas_call x1, Pallas kernels: 62.8 us -> 61.7 us  [in_one_kernel(): pl.pallas_call(kernel, out_shape=(jax.ShapeDtypeStruct((1, n_rows), f32),...]
where the time goes in v3:
time: 75.9 us; the launch traced here: 75.7 us
  Pallas kernels  74.9 us (99%)
  between operations  0.8 us (1%)
    pallas_call x1, Pallas kernels, in_one_kernel(): pl.pallas_call(kernel, out_shape=(jax.ShapeDtypeStruct((1, n_rows), f32),...  61.7 us
    pallas_call x1, Pallas kernels, in_one_kernel(): pl.pallas_call(write_out, out_shape=tuple((jax.ShapeDtypeStruct(out.shape...  13.3 us

profile of v3, /device:TPU:0, one launch (start us, length us, event | category | flops | bytes accessed | tf_op | source)
XLA Modules:
  0.0 75.7 jit_solution(2996106348169306549)
XLA Ops:
  0.6 61.7 %lloyd_step.1 = (f32[1,1024]{1,0:T(1,128)}, f32[128,768]{1,0:T(8,128)}, f32[1,1024]{1,0:T(1,128)}) custom-call(bf16[1024,768]{1,0:T(8,128)(2,1)} %emb.1, bf16[128,768]{1,0:T(8,128)(2,1)} %cen.1, s32[8,128]{1,0:T(8,128)} %bitcast.3), custom_call_target="tpu_custom_call" | custom-call | flops 9663676416 | bytes 6291456 | tf_op jit(solution)/shard_map/lloyd_step/pallas_call | solution.py:308
  62.3 13.3 %write_out.1 = (f32[1,1024]{1,0:T(1,128)}, f32[128,768]{1,0:T(8,128)}, f32[1,1024]{1,0:T(1,128)}) custom-call(f32[1,1024]{1,0:T(1,128)} %get-tuple-element.9.old_min, f32[128,768]{1,0:T(8,128)} %get-tuple-element.10.refined, f32[1,1024]{1,0:T(1,128)} %get-tuple-element.11.new_min), custom_call_target="tpu_custom_call" | custom-call | tf_op jit(solution)/shard_map/write_out/pallas_call | solution.py:356

commit v4 on v3

--- a/solution.py
+++ b/solution.py
@@ -168,10 +168,9 @@
 
     own_lab.wait()
     own_rows.wait()
-    rows_in.wait_recv()
-    labels_in.wait_recv()
-
-    def partial(j, fa):
+    old.along_z(1)
+
+    def partial(j, fa, first=False):
         hot = []
         for fb in range(2):
             xa = x + fa * (x1 - x) + fb * (x2 - x)
@@ -188,12 +187,15 @@
             return part + jnp.dot(block, rows[g], preferred_element_type=jnp.float32)
 
         part = one(0, jnp.zeros((2 * owned, half + 128), jnp.float32))
+        if first:
+            rows_in.wait_recv()
+            labels_in.wait_recv()
         return one(1, part)
 
     stage1, stage2, stage3 = {}, {}, {}
 
     def begin(j):
-        part = partial(j, 1)
+        part = partial(j, 1, j == SLICES[0])
         for fb in range(2):
             pack(part[fb * owned : (fb + 1) * owned], out1.at[j, fb], meta1.at[j, fb])
         stage1[j] = (send(out1.at[j], in1.at[j], p1), send(meta1.at[j], min1.at[j], p1))
@@ -218,25 +220,29 @@
             stage3[j] = (send(out3.at[i], in3.at[i], above[j]), send(meta3.at[i], min3.at[i], above[j]))
 
     begin(SLICES[0])
+    old.along_z(2, 3)
     begin(SLICES[1])
-    old.along_z(1, 2, 3)
+    middle(SLICES[0])
     own_emb.wait()
     wide = here[...]
     scaled[...] = wide * jnp.asarray(-2.0, jnp.bfloat16)
     norms[...] = square_sums(wide)[0:8, :]
 
-    middle(SLICES[0])
     begin(SLICES[2])
     middle(SLICES[1])
     settle(SLICES[0])
+    old.along_d1(0, 1)
     begin(SLICES[3])
     middle(SLICES[2])
     settle(SLICES[1])
-    old.along_d1(0, 1, 2, 3)
+    old.along_d1(2, 3)
     middle(SLICES[3])
     settle(SLICES[2])
+    own_old.wait()
+    old.need(old.fz)
+    nearest(old_all, old_acc, y, x)
+    old.along_d2(0, 1, 2, 3)
     settle(SLICES[3])
-    old.along_d2(0, 1, 2, 3)
 
     total = tot[0]
     for j in SLICES[:3]:
@@ -251,9 +257,6 @@
     new = Gather(mine, new_all, True)
     half_in = send(halves.at[c], halves.at[c], sib)
 
-    own_old.wait()
-    old.need(old.fz)
-    nearest(old_all, old_acc, y, x)
     new.along_z(1)
     old.last(0, 1, 2, 3)
     new.along_z(2)
@@ -288,15 +291,6 @@
 
 
 COPIES = 96
-
-
-def write_out(old_min, refined, new_min, old_out, refined_out, new_out, sems):
-    pairs = ((old_min, old_out), (refined, refined_out), (new_min, new_out))
-    copies = [pltpu.make_async_copy(src, dst, sems.at[i]) for i, (src, dst) in enumerate(pairs)]
-    for copy in copies:
-        copy.start()
-    for copy in copies:
-        copy.wait()
 
 
 def in_one_kernel(embeddings, centers, assignment):
@@ -351,17 +345,6 @@
         ),
         name="lloyd_step",
     )(embeddings, centers, assignment.reshape(n_rows // 128, 128))
-    outs = (old_min, refined, new_min)
-    anywhere = pl.BlockSpec(memory_space=pl.ANY)
-    old_min, refined, new_min = pl.pallas_call(
-        write_out,
-        out_shape=tuple(jax.ShapeDtypeStruct(out.shape, f32) for out in outs),
-        in_specs=[anywhere] * 3,
-        out_specs=(anywhere,) * 3,
-        scratch_shapes=[pltpu.SemaphoreType.DMA((3,))],
-        compiler_params=pltpu.CompilerParams(vmem_limit_bytes=60 * 1024 * 1024),
-        name="write_out",
-    )(*outs)
     return old_min.reshape(n_rows), refined, new_min.reshape(n_rows)
 
 

time: 75.9 us -> 69 us (0.909)
  Pallas kernels: 74.9 us -> 63.8 us
  local copies, waits for them, and re-layouts: 0 us -> 4.3 us
    pallas_call x1 -> x0, Pallas kernels: 13.3 us -> none  [in_one_kernel(): pl.pallas_call(write_out, out_shape=tuple((jax.ShapeDtypeStruct(out.shape...]
    unnamed x0 -> x3, local copies, waits for them, and re-layouts: none -> 4.3 us
    pallas_call x1, Pallas kernels: 61.7 us -> 63.8 us  [in_one_kernel(): pl.pallas_call(kernel, out_shape=(jax.ShapeDtypeStruct((1, n_rows), f32),...]
where the time goes in v4:
time: 69 us; the launch traced here: 68.7 us
  Pallas kernels  63.8 us (92%)
  local copies, waits for them, and re-layouts  4.3 us (6%)
    pallas_call x1, Pallas kernels, in_one_kernel(): pl.pallas_call(kernel, out_shape=(jax.ShapeDtypeStruct((1, n_rows), f32),...  63.8 us
    unnamed x3, local copies, waits for them, and re-layouts  4.3 us

profile of v4, /device:TPU:0, one launch (start us, length us, event | category | flops | bytes accessed | tf_op | source)
XLA Modules:
  0.0 68.7 jit_solution(3124407367854603106)
XLA Ops:
  0.6 63.8 %lloyd_step.1 = (f32[1,1024]{1,0:T(1,128)}, f32[128,768]{1,0:T(8,128)}, f32[1,1024]{1,0:T(1,128)}) custom-call(bf16[1024,768]{1,0:T(8,128)(2,1)} %emb.1, bf16[128,768]{1,0:T(8,128)(2,1)} %cen.1, s32[8,128]{1,0:T(8,128)} %bitcast.5), custom_call_target="tpu_custom_call" | custom-call | flops 9663676416 | bytes 6291456 | tf_op jit(solution)/shard_map/lloyd_step/pallas_call | solution.py:302
  64.4 1.3 %copy.9 = f32[1024]{0:T(1024)} copy(f32[1024]{0:T(1024)} %bitcast.4) | data formatting | bytes 8192
  65.7 1.8 %copy.10 = f32[128,768]{1,0:T(8,128)} copy(f32[128,768]{1,0:T(8,128)} %get-tuple-element.13) | data formatting | bytes 786432
  67.5 1.3 %copy.11 = f32[1024]{0:T(1024)} copy(f32[1024]{0:T(1024)} %bitcast.3) | data formatting | bytes 8192

commit v5 on v4

--- a/solution.py
+++ b/solution.py
@@ -168,7 +168,6 @@
 
     own_lab.wait()
     own_rows.wait()
-    old.along_z(1)
 
     def partial(j, fa, first=False):
         hot = []
@@ -220,8 +219,8 @@
             stage3[j] = (send(out3.at[i], in3.at[i], above[j]), send(meta3.at[i], min3.at[i], above[j]))
 
     begin(SLICES[0])
-    old.along_z(2, 3)
     begin(SLICES[1])
+    old.along_z(1, 2, 3)
     middle(SLICES[0])
     own_emb.wait()
     wide = here[...]
@@ -231,18 +230,17 @@
     begin(SLICES[2])
     middle(SLICES[1])
     settle(SLICES[0])
-    old.along_d1(0, 1)
     begin(SLICES[3])
     middle(SLICES[2])
     settle(SLICES[1])
-    old.along_d1(2, 3)
+    old.along_d1(0, 1, 2, 3)
     middle(SLICES[3])
     settle(SLICES[2])
     own_old.wait()
     old.need(old.fz)
     nearest(old_all, old_acc, y, x)
+    settle(SLICES[3])
     old.along_d2(0, 1, 2, 3)
-    settle(SLICES[3])
 
     total = tot[0]
     for j in SLICES[:3]:
@@ -338,7 +336,7 @@
             pltpu.SemaphoreType.DMA((COPIES,)),
         ],
         compiler_params=pltpu.CompilerParams(
-            collective_id=0, has_side_effects=True, vmem_limit_bytes=60 * 1024 * 1024
+            collective_id=0, has_side_effects=True, vmem_limit_bytes=53 * 1024 * 1024
         ),
         cost_estimate=pl.CostEstimate(
             flops=6 * n_rows * 16 * owned * width, bytes_accessed=8 * n_rows * width, transcendentals=0

time: 69 us -> 64.8 us (0.939)
  Pallas kernels: 63.8 us -> 60.5 us
  local copies, waits for them, and re-layouts: 4.3 us -> 3.54 us
    pallas_call x1, Pallas kernels: 63.8 us -> 60.5 us  [in_one_kernel(): pl.pallas_call(kernel, out_shape=(jax.ShapeDtypeStruct((1, n_rows), f32),...]
    unnamed x3 -> x7, local copies, waits for them, and re-layouts: 4.3 us -> 3.54 us
where the time goes in v5:
time: 64.8 us; the launch traced here: 64.6 us
  Pallas kernels  60.5 us (93%)
  local copies, waits for them, and re-layouts  3.54 us (5%)
  between operations  0.65 us (1%)
    pallas_call x1, Pallas kernels, in_one_kernel(): pl.pallas_call(kernel, out_shape=(jax.ShapeDtypeStruct((1, n_rows), f32),...  60.5 us
    unnamed x7, local copies, waits for them, and re-layouts  3.54 us

profile of v5, /device:TPU:0, one launch (start us, length us, event | category | flops | bytes accessed | tf_op | source)
XLA Modules:
  0.0 64.6 jit_solution(12399737504558739374)
XLA Ops:
  0.6 0.0 copy-start
  0.6 0.9 %copy-done = bf16[128,768]{1,0:T(8,128)(2,1)S(1)} copy-done((bf16[128,768]{1,0:T(8,128)(2,1)S(1)}, bf16[128,768]{1,0:T(8,128)(2,1)}, u32[]{:S(2)}) %copy-start) | copy-done | bytes 196632
  1.6 0.0 copy-start.1
  1.6 0.7 %copy-done.1 = s32[1024,1]{0,1:T(1,128)S(1)} copy-done((s32[1024,1]{0,1:T(1,128)S(1)}, s32[1024,1]{0,1:T(1,128)}, u32[]{:S(2)}) %copy-start.1) | copy-done | bytes 4120
  2.2 60.5 %lloyd_step.1 = (f32[1,1024]{1,0:T(1,128)S(1)}, f32[128,768]{1,0:T(8,128)S(1)}, f32[1,1024]{1,0:T(1,128)S(1)}) custom-call(bf16[1024,768]{1,0:T(8,128)(2,1)} %emb.1, bf16[128,768]{1,0:T(8,128)(2,1)S(1)} %copy-done, s32[8,128]{1,0:T(8,128)S(1)} %bitcast.5), custom_call_target="tpu_custom_call" | custom-call | flops 9663676416 | bytes 6291456 | tf_op jit(solution)/shard_map/lloyd_step/pallas_call | solution.py:300
  62.7 0.6 copy.9
  63.3 0.7 %copy.10 = f32[128,768]{1,0:T(8,128)} copy(f32[128,768]{1,0:T(8,128)S(1)} %get-tuple-element.13) | data formatting | bytes 786432
  64.0 0.6 copy.11
Async XLA Ops:
  0.6 0.9 %copy-start = (bf16[128,768]{1,0:T(8,128)(2,1)S(1)}, bf16[128,768]{1,0:T(8,128)(2,1)}, u32[]{:S(2)}) copy-start(bf16[128,768]{1,0:T(8,128)(2,1)} %cen.1) | copy-start | bytes 589828
  1.6 0.7 %copy-start.1 = (s32[1024,1]{0,1:T(1,128)S(1)}, s32[1024,1]{0,1:T(1,128)}, u32[]{:S(2)}) copy-start(s32[1024,1]{0,1:T(1,128)} %param.5) | copy-start | bytes 12292

commit v6 on v5

--- a/solution.py
+++ b/solution.py
@@ -220,7 +220,6 @@
 
     begin(SLICES[0])
     begin(SLICES[1])
-    old.along_z(1, 2, 3)
     middle(SLICES[0])
     own_emb.wait()
     wide = here[...]
@@ -229,6 +228,7 @@
 
     begin(SLICES[2])
     middle(SLICES[1])
+    old.along_z(1, 2, 3)
     settle(SLICES[0])
     begin(SLICES[3])
     middle(SLICES[2])
@@ -256,12 +256,12 @@
     half_in = send(halves.at[c], halves.at[c], sib)
 
     new.along_z(1)
-    old.last(0, 1, 2, 3)
     new.along_z(2)
     old.need(old.f1 + old.f2)
     nearest(old_all, old_acc, y1, x1)
     new.along_z(3)
     new.along_d1(0, 1)
+    old.last(0, 1, 2, 3)
     nearest(old_all, old_acc, y2, x2)
     new.along_d1(2, 3)
     new.along_d2(0, 1, 2, 3)

time: 64.8 us -> 67.1 us (1.035)
  Pallas kernels: 60.5 us -> 62.7 us
    pallas_call x1, Pallas kernels: 60.5 us -> 62.7 us  [in_one_kernel(): pl.pallas_call(kernel, out_shape=(jax.ShapeDtypeStruct((1, n_rows), f32),...]
where the time goes in v6:
time: 67.1 us; the launch traced here: 66.9 us
  Pallas kernels  62.7 us (93%)
  local copies, waits for them, and re-layouts  3.54 us (5%)
    pallas_call x1, Pallas kernels, in_one_kernel(): pl.pallas_call(kernel, out_shape=(jax.ShapeDtypeStruct((1, n_rows), f32),...  62.7 us
    unnamed x7, local copies, waits for them, and re-layouts  3.54 us

profile of v6, /device:TPU:0, one launch (start us, length us, event | category | flops | bytes accessed | tf_op | source)
XLA Modules:
  0.0 66.9 jit_solution(15094046768734635993)
XLA Ops:
  0.6 0.0 copy-start
  0.6 0.9 %copy-done = bf16[128,768]{1,0:T(8,128)(2,1)S(1)} copy-done((bf16[128,768]{1,0:T(8,128)(2,1)S(1)}, bf16[128,768]{1,0:T(8,128)(2,1)}, u32[]{:S(2)}) %copy-start) | copy-done | bytes 196632
  1.6 0.0 copy-start.1
  1.6 0.7 %copy-done.1 = s32[1024,1]{0,1:T(1,128)S(1)} copy-done((s32[1024,1]{0,1:T(1,128)S(1)}, s32[1024,1]{0,1:T(1,128)}, u32[]{:S(2)}) %copy-start.1) | copy-done | bytes 4120
  2.2 62.7 %lloyd_step.1 = (f32[1,1024]{1,0:T(1,128)S(1)}, f32[128,768]{1,0:T(8,128)S(1)}, f32[1,1024]{1,0:T(1,128)S(1)}) custom-call(bf16[1024,768]{1,0:T(8,128)(2,1)} %emb.1, bf16[128,768]{1,0:T(8,128)(2,1)S(1)} %copy-done, s32[8,128]{1,0:T(8,128)S(1)} %bitcast.5), custom_call_target="tpu_custom_call" | custom-call | flops 9663676416 | bytes 6291456 | tf_op jit(solution)/shard_map/lloyd_step/pallas_call | solution.py:300
  65.0 0.6 copy.9
  65.6 0.7 %copy.10 = f32[128,768]{1,0:T(8,128)} copy(f32[128,768]{1,0:T(8,128)S(1)} %get-tuple-element.13) | data formatting | bytes 786432
  66.3 0.6 copy.11
Async XLA Ops:
  0.6 0.9 %copy-start = (bf16[128,768]{1,0:T(8,128)(2,1)S(1)}, bf16[128,768]{1,0:T(8,128)(2,1)}, u32[]{:S(2)}) copy-start(bf16[128,768]{1,0:T(8,128)(2,1)} %cen.1) | copy-start | bytes 589828
  1.6 0.7 %copy-start.1 = (s32[1024,1]{0,1:T(1,128)S(1)}, s32[1024,1]{0,1:T(1,128)}, u32[]{:S(2)}) copy-start(s32[1024,1]{0,1:T(1,128)} %param.5) | copy-start | bytes 12292
